TPU v7x, 32 devices: a whole 2x2x4 slice. The times are simulated.
32 devices in a mesh: grp: 2 (over y), run: 4 (over x, core), chan: 4 (over z).
Axes of the slice: x: 2, y: 2, z: 4, core: 2. Of those that a mesh axis runs over, the one named last changes fastest.
Arguments:
- embed: bfloat16 [512, 8192], P('grp', 'chan'), parts along dimension 0, may hold values from -6 to 6
- noise: bfloat16 [16, 32, 8192], P(('grp', 'run'), None, 'chan'), parts along dimension 0, may hold values from -12 to 12
- positions: int32 [16, 32], P(('grp', 'run')), parts along dimension 0, may hold values from 0 to 255
- restore: int32 [16, 2], P(('grp', 'run')), parts along dimension 0, may hold values 0 or 1
- short_one: float32 [7, 8192], P(None, 'chan'), may hold values from -2 to 2
- long_one: float32 [128, 8192], P(None, 'chan'), may hold values from -0.5 to 0.5
- out_weight: bfloat16 [8192, 8192], P(None, 'chan'), may hold values from -0.0625 to 0.0625
- short_two: float32 [7, 8192], P(None, 'chan'), may hold values from -2 to 2
- long_two: float32 [128, 8192], P(None, 'chan'), may hold values from -0.5 to 0.5
Outputs:
- traced: bfloat16 [16, 256, 8192], P(('grp', 'run'), None, 'chan'), parts along dimension 0
There are 2 independent parts, one for each index of `grp`. A program takes and returns all parts, laid end to end along the dimension named above; an argument that names none is the same for every part. Nothing has to cross between parts.
All inputs are finite; a program needn't handle non-finite values. No bound on the sum of `restore` on one device may be relied on, other than what follows from the above.
Results may differ from a plain program's by a relative error of at most 0.007.
Values may be sent and summed in bfloat16 or wider, within the bound.
A program may use at most 128 MiB of HBM per device.

v0:
```python
import jax
import jax.numpy as jnp
from jax import lax
from jax.sharding import PartitionSpec as P


def short_filter(field, filter_taps):
    length = field.shape[1]
    running = jnp.zeros(field.shape, jnp.float32)
    for shift_count in range(filter_taps.shape[0]):
        shifted = jnp.pad(field, ((0, 0), (shift_count, 0), (0, 0)))[:, :length]
        running = running + filter_taps[shift_count][None, None, :] * shifted
    return running


def block_filter(field, filter_taps):
    width = field.shape[2]
    span = filter_taps.shape[0]
    kernel = filter_taps[::-1][:, None, :]
    return lax.conv_general_dilated(
        field,
        kernel,
        window_strides=(1,),
        padding=((span - 1, 0),),
        dimension_numbers=("NWC", "WIO", "NWC"),
        feature_group_count=width,
        precision=lax.Precision.HIGHEST,
        preferred_element_type=jnp.float32,
    )


def per_device(
    embed, noise, positions, restore, short_one, long_one, out_weight, short_two, long_two
):
    run_count = noise.shape[0]
    length = embed.shape[0]
    first_run = lax.axis_index("run") * run_count
    run_ids = first_run + jnp.arange(run_count, dtype=jnp.int32)
    onehot = (jnp.arange(length, dtype=jnp.int32)[None, :, None] == positions[:, None, :]).astype(
        jnp.bfloat16
    )
    added = jnp.einsum("rlp,rpc->rlc", onehot, noise, preferred_element_type=jnp.float32)
    corrupt_flag = (run_ids != 0).astype(jnp.float32)[:, None, None]
    inputs = (embed.astype(jnp.float32)[None] + corrupt_flag * added).astype(jnp.bfloat16)
    batch_inputs = jnp.concatenate([inputs, embed[None]], axis=0)
    input_values = batch_inputs.astype(jnp.float32)
    filtered = block_filter(short_filter(input_values, short_one), long_one)
    mixed = (filtered * jax.nn.silu(input_values)).astype(jnp.bfloat16)
    initial = jnp.zeros((mixed.shape[0], length, out_weight.shape[1]), jnp.float32)
    segment = lax.all_gather(mixed, "chan", axis=2, tiled=True)
    weight_rows = lax.slice_in_dim(out_weight, 0, segment.shape[2], axis=0)
    projected = initial + jnp.einsum(
        "rlk,kc->rlc", segment, weight_rows, preferred_element_type=jnp.float32
    )
    hidden = (input_values + projected).astype(jnp.bfloat16)
    clean_hidden = hidden[run_count]
    hidden = hidden[:run_count]
    block_size = length // restore.shape[1]
    restored_rows = jnp.repeat(restore, block_size, axis=1)[:, :, None] == 1
    restored = jnp.where(restored_rows, clean_hidden[None], hidden)
    restored_values = restored.astype(jnp.float32)
    second = block_filter(short_filter(restored_values, short_two), long_two)
    return (restored_values + second * jax.nn.silu(restored_values)).astype(jnp.bfloat16)


def solution(mesh):
    in_specs = (
        P("grp", "chan"),
        P(("grp", "run"), None, "chan"),
        P(("grp", "run"), None),
        P(("grp", "run"), None),
        P(None, "chan"),
        P(None, "chan"),
        P(None, "chan"),
        P(None, "chan"),
        P(None, "chan"),
    )
    out_specs = P(("grp", "run"), None, "chan")
    return jax.shard_map(
        per_device, mesh=mesh, in_specs=in_specs, out_specs=out_specs, check_vma=False
    )
```

profile of v0, /device:TPU:0, one launch (start us, length us, event | category | flops | bytes accessed | tf_op | source)
XLA Modules:
  0.0 446.8 jit_solution(15623138889471099007)
XLA Ops:
  6.5 0.0 copy-start
  6.5 0.0 all-gather.2.cloned.1.call-start
  6.5 1.2 fusion.40
  7.8 0.0 copy-start.2
  7.8 2.9 convert_element_type.53
  10.7 8.9 %rev.6 = f32[128,2048]{1,0:T(8,128)} reverse(f32[128,2048]{1,0:T(8,128)} %param.14), dimensions={0} | reverse | bytes 2097152 | tf_op jit(solution)/shard_map/rev | solution.py:19
  19.5 0.0 copy-done
  19.5 0.0 copy-done.6
  19.5 2.4 add_convert_fusion.1
  22.0 0.0 copy-done.2
  22.0 0.4 maximum_convert_fusion
  22.4 0.0 copy-start.4
  22.4 5.2 %fusion.10 = f32[3,256,2048]{2,1,0:T(8,128)S(1)} fusion(f32[3,256,2048]{2,1,0:T(8,128)S(1)} %maximum_convert_fusion, f32[2048]{0:T(1024)S(1)} %bitcast.48, f32[2048]{0:T(1024)S(1)} %bitcast.49, f32[2048]{0:T(1024)S(1)} %bitcast.44, f32[2048]{0:T(1024)S(1)} %bitcast.45, f32[2048]{0:T(1024)S(1)} %bitcast.46, f32[2048]{0:T(1024)S(1)} %bitcast.47, ...), kind=kLoop, calls=%fused_computation.16 | loop fusion | flops 20447232 | bytes 12640256 | tf_op jit(solution)/shard_map/add | solution.py:12
  27.6 0.0 copy-done.4
  27.6 98.9 %fusion.2 = f32[3,256,2048]{2,0,1:T(4,128)S(1)} fusion(f32[3,256,2048]{2,1,0:T(8,128)S(1)} %fusion.10, f32[128,1,2048]{2,0,1:T(8,128)S(1)} %bitcast.35), kind=kOutput, calls=%fused_computation.2 | convolution fusion | flops 1816657920 | bytes 13631488 | tf_op jit(solution)/shard_map/conv_general_dilated | solution.py:20
  126.5 0.0 copy-start.7
  126.5 5.2 %fusion.16 = bf16[3,256,2048]{2,1,0:T(8,128)(2,1)} fusion(f32[3,256,2048]{2,0,1:T(4,128)S(1)} %fusion.2, bf16[1,256,2048]{2,1,0:T(8,128)(2,1)S(1)} %bitcast.32, bf16[2,256,2048]{2,1,0:T(8,128)(2,1)S(1)} %add_convert_fusion.1), kind=kLoop, calls=%fused_computation.23 | loop fusion | flops 12582912 | bytes 12582912 | tf_op jit(solution)/shard_map/convert_element_type | solution.py:48
  131.7 0.0 all-gather.2.cloned.1.call-update
  131.8 0.0 copy-done.7
  131.8 0.1 broadcast_bitcast_fusion
  131.9 8.9 %rev.7 = f32[128,2048]{1,0:T(8,128)} reverse(f32[128,2048]{1,0:T(8,128)} %param.17), dimensions={0} | reverse | bytes 2097152 | tf_op jit(solution)/shard_map/rev | solution.py:19
  140.7 0.0 copy-done.5
  140.8 212.0 %all-gather.2.cloned.1.call-done = bf16[3,256,8192]{2,1,0:T(8,128)(2,1)} async-done(((bf16[3,256,2048]{2,1,0:T(8,128)(2,1)}), bf16[3,256,8192]{2,1,0:T(8,128)(2,1)}) %all-gather.2.cloned.1.call-update) | async-done | bytes 12582928 | tf_op jit(solution)/shard_map/all_gather | solution.py:50
  352.8 33.6 %add_convert_fusion = bf16[3,256,2048]{2,1,0:T(8,128)(2,1)S(1)} fusion(bf16[3,256,8192]{2,1,0:T(8,128)(2,1)} %all-gather.2.cloned.1.call-done, bf16[8192,2048]{1,0:T(8,128)(2,1)} %param.15, bf16[1,256,2048]{2,1,0:T(8,128)(2,1)S(1)} %bitcast.33, bf16[2,256,2048]{2,1,0:T(8,128)(2,1)S(1)} %add_convert_fusion.1), kind=kOutput, calls=%fused_computation.24 | convolution fusion | flops 25776095232 | bytes 52428800 | tf_op jit(solution)/shard_map/rlk,kc->rlc/dot_general | solution.py:52
  386.5 0.1 slice_bitcast_fusion
  386.6 0.4 fusion.35
  386.9 0.0 copy-start.3
  386.9 3.5 fusion.23
  390.4 0.0 copy-done.3
  390.4 0.0 copy-start.1
  390.4 45.4 %fusion.31 = f32[2,256,2048]{2,0,1:T(2,128)S(1)} fusion(f32[2,256,2048]{2,1,0:T(8,128)S(1)} %fusion.23, f32[128,1,2048]{2,0,1:T(8,128)S(1)} %bitcast.34), kind=kOutput, calls=%fused_computation.46 | convolution fusion | flops 1211105280 | bytes 9437184 | tf_op jit(solution)/shard_map/conv_general_dilated | solution.py:20
  435.9 4.1 fusion.30
  (7 shorter events, 0.1 us)
Async XLA Ops:
  6.5 13.0 %copy-start = (bf16[2,32,2048]{2,1,0:T(8,128)(2,1)S(1)}, bf16[2,32,2048]{2,1,0:T(8,128)(2,1)}, u32[]{:S(2)}) copy-start(bf16[2,32,2048]{2,1,0:T(8,128)(2,1)} %param.10) | copy-start | bytes 786436
  6.5 13.0 %copy-start.6 = (s32[2,32]{1,0:T(2,128)S(1)}, s32[2,32]{1,0:T(2,128)}, u32[]{:S(2)}) copy-start(s32[2,32]{1,0:T(2,128)} %param.11) | copy-start | bytes 772
  6.5 346.3 %all-gather.2.cloned.1.call-start = ((), (), s32[]{:S(2)}) async-start(), calls=%async_computation | async-start | bytes 15728640 | tf_op jit(solution)/shard_map/all_gather | solution.py:50
  7.8 14.2 %copy-start.2 = (bf16[256,2048]{1,0:T(8,128)(2,1)S(1)}, bf16[256,2048]{1,0:T(8,128)(2,1)}, u32[]{:S(2)}) copy-start(bf16[256,2048]{1,0:T(8,128)(2,1)} %param.9) | copy-start | bytes 3145732
  22.4 5.2 %copy-start.4 = (f32[128,2048]{1,0:T(8,128)S(1)}, f32[128,2048]{1,0:T(8,128)}, u32[]{:S(2)}) copy-start(f32[128,2048]{1,0:T(8,128)} %rev.6) | copy-start | bytes 3145732
  126.5 5.3 %copy-start.7 = (s32[2,2]{1,0:T(2,128)S(1)}, s32[2,2]{1,0:T(2,128)}, u32[]{:S(2)}) copy-start(s32[2,2]{1,0:T(2,128)} %param.12) | copy-start | bytes 52
  131.7 9.0 %copy-start.5 = (f32[7,2048]{1,0:T(8,128)S(1)}, f32[7,2048]{1,0:T(8,128)}, u32[]{:S(2)}) copy-start(f32[7,2048]{1,0:T(8,128)} %param.16) | copy-start | bytes 172036
  386.9 3.5 copy-start.3
  390.4 49.5 %copy-start.1 = (bf16[2,32,2048]{2,1,0:T(8,128)(2,1)S(1)}, bf16[2,32,2048]{2,1,0:T(8,128)(2,1)}, u32[]{:S(2)}) copy-start(bf16[2,32,2048]{2,1,0:T(8,128)(2,1)} %param.10) | copy-start | bytes 786436
Sparse Core Ops, SparseCore 0:
  131.9 220.8 all-gather.1
where the time goes:
time: 448 us; the launch traced here: 447 us
  waiting for transfers between devices  212 us (47%)
  matrix products  180 us (40%)
  other arithmetic  21.6 us (5%)
  local copies, waits for them, and re-layouts  19.2 us (4%)
  between operations  13.6 us (3%)
    all_gather x1, waiting for transfers between devices, per_device(): segment = lax.all_gather(mixed, 'chan', axis=2, tiled=True)  212 us
    conv_general_dilated x2, matrix products, block_filter(): lax.conv_general_dilated(field, kernel, window_strides=(1,), padding=((sp...  144 us
    dot_general x1, matrix products, per_device(): jnp.einsum('rlk,kc->rlc', segment, weight_rows, preferred_element_type=jn...  33.6 us
    rev x2, local copies, waits for them, and re-layouts, block_filter(): kernel = filter_taps[::-1][:, None, :]  17.7 us
  transfers between devices with their start and end apart: 1, of which 1 were waited for; matrix products, arithmetic and copies ran while one was open for 2% of the time, Pallas kernels for 0%

commit v1 on v0

--- a/solution.py
+++ b/solution.py
@@ -2,6 +2,19 @@
 import jax.numpy as jnp
 from jax import lax
 from jax.sharding import PartitionSpec as P
+from jax.lax import axis_index, axis_size, ppermute
+
+
+def run_zone(local_array):
+    nodes = axis_size("chan")
+    kept_rows = [(to_i, (to_i + 1) % nodes) for to_i in range(nodes)]
+    part_next = [None] * nodes
+    part_next[nodes - 1] = local_array
+    for c in range(nodes - 2, -1, -1):
+        part_next[c] = ppermute(part_next[c + 1], "chan", kept_rows)
+    newest = jnp.concatenate(part_next, axis=2)
+    local_next = (axis_index("chan") + 1) * local_array.shape[2]
+    return jnp.roll(newest, local_next, axis=2)
 
 
 def short_filter(field, filter_taps):
@@ -47,7 +60,7 @@
     filtered = block_filter(short_filter(input_values, short_one), long_one)
     mixed = (filtered * jax.nn.silu(input_values)).astype(jnp.bfloat16)
     initial = jnp.zeros((mixed.shape[0], length, out_weight.shape[1]), jnp.float32)
-    segment = lax.all_gather(mixed, "chan", axis=2, tiled=True)
+    segment = run_zone(mixed)
     weight_rows = lax.slice_in_dim(out_weight, 0, segment.shape[2], axis=0)
     projected = initial + jnp.einsum(
         "rlk,kc->rlc", segment, weight_rows, preferred_element_type=jnp.float32

time: 448 us -> 457 us (1.020)
  local copies, waits for them, and re-layouts: 19.2 us -> 45.9 us
  between operations: 13.6 us -> 0.21 us
  waiting for transfers between devices: 212 us -> 203 us
    all_gather x1 -> x0, waiting for transfers between devices: 212 us -> none  [per_device(): segment = lax.all_gather(mixed, 'chan', axis=2, tiled=True)]
    ppermute x0 -> x3, waiting for transfers between devices: none -> 203 us  [run_zone(): part_next[c] = ppermute(part_next[c + 1], 'chan', kept_rows)]
    unnamed x18 -> x37, local copies, waits for them, and re-layouts: 0.12 us -> 24.9 us
    conv_general_dilated x2, matrix products: 144 us -> 149 us  [block_filter(): lax.conv_general_dilated(field, kernel, window_strides=(1,), padding=((sp...]
  transfers between devices with their start and end apart: 1 -> 3, of which waited for: 1 -> 3; matrix products, arithmetic and copies ran while one was open for 2% -> 2% of each run, Pallas kernels for 0% -> 0%
where the time goes in v1:
time: 457 us; the launch traced here: 456 us
  waiting for transfers between devices  203 us (44%)
  matrix products  184 us (40%)
  local copies, waits for them, and re-layouts  45.9 us (10%)
  other arithmetic  20.4 us (4%)
    ppermute x3, waiting for transfers between devices, run_zone(): part_next[c] = ppermute(part_next[c + 1], 'chan', kept_rows)  203 us
    conv_general_dilated x2, matrix products, block_filter(): lax.conv_general_dilated(field, kernel, window_strides=(1,), padding=((sp...  149 us
    dot_general x1, matrix products, per_device(): jnp.einsum('rlk,kc->rlc', segment, weight_rows, preferred_element_type=jn...  33.7 us
    unnamed x37, local copies, waits for them, and re-layouts  24.9 us
    rev x2, local copies, waits for them, and re-layouts, block_filter(): kernel = filter_taps[::-1][:, None, :]  17.8 us
    add x2, other arithmetic, short_filter(): running = running + filter_taps[shift_count][None, None, :] * shifted  9.79 us
  transfers between devices with their start and end apart: 3, of which 3 were waited for; matrix products, arithmetic and copies ran while one was open for 2% of the time, Pallas kernels for 0%

profile of v1, /device:TPU:0, one launch (start us, length us, event | category | flops | bytes accessed | tf_op | source)
XLA Modules:
  0.0 455.9 jit_solution(7375964857474336920)
XLA Ops:
  0.0 1.2 fusion.44
  1.2 0.0 copy-start.6
  1.2 1.5 convert_element_type.53
  2.8 8.9 %rev.6 = f32[128,2048]{1,0:T(8,128)} reverse(f32[128,2048]{1,0:T(8,128)} %param.14), dimensions={0} | reverse | bytes 2097152 | tf_op jit(solution)/shard_map/rev | solution.py:32
  11.7 0.8 add_convert_fusion.1
  12.6 0.4 maximum_convert_fusion
  13.0 6.3 %fusion.11 = f32[3,256,2048]{2,1,0:T(8,128)} fusion(f32[3,256,2048]{2,1,0:T(8,128)S(1)} %maximum_convert_fusion, f32[2048]{0:T(1024)S(1)} %bitcast.47, f32[2048]{0:T(1024)S(1)} %bitcast.48, f32[2048]{0:T(1024)S(1)} %bitcast.43, f32[2048]{0:T(1024)S(1)} %bitcast.44, f32[2048]{0:T(1024)S(1)} %bitcast.45, f32[2048]{0:T(1024)S(1)} %bitcast.46, f32[2048]{0:T(1024)S(1)} %bitcast.42), kind=kLoop, calls=%fused_computation.17 | loop fusion | flops 20447232 | bytes 12640256 | tf_op jit(solution)/shard_map/add | solution.py:25
  19.4 103.7 %fusion.3 = f32[3,256,2048]{2,0,1:T(4,128)S(1)} fusion(f32[3,256,2048]{2,1,0:T(8,128)} %fusion.11, f32[128,1,2048]{2,0,1:T(8,128)S(1)} %bitcast.34), kind=kOutput, calls=%fused_computation.3 | convolution fusion | flops 1816657920 | bytes 13631488 | tf_op jit(solution)/shard_map/conv_general_dilated | solution.py:33
  123.1 4.1 fusion.17
  127.2 3.1 collective-permute-start
  130.3 70.1 %collective-permute-done = bf16[3,256,2048]{2,1,0:T(8,128)(2,1)S(1)} collective-permute-done((bf16[3,256,2048]{2,1,0:T(8,128)(2,1)S(1)}, bf16[3,256,2048]{2,1,0:T(8,128)(2,1)S(1)}, u32[]{:S(2)}, u32[]{:S(2)}) %collective-permute-start) | collective-permute-done | bytes 3145760 | tf_op jit(solution)/shard_map/ppermute | solution.py:14
  200.4 1.6 copy-done.4
  202.1 71.2 %collective-permute-done.1 = bf16[3,256,2048]{2,1,0:T(8,128)(2,1)} collective-permute-done((bf16[3,256,2048]{2,1,0:T(8,128)(2,1)S(1)}, bf16[3,256,2048]{2,1,0:T(8,128)(2,1)}, u32[]{:S(2)}, u32[]{:S(2)}) %collective-permute-start.1) | collective-permute-done | bytes 3145760 | tf_op jit(solution)/shard_map/ppermute | solution.py:14
  273.3 0.1 broadcast_bitcast_fusion
  273.4 8.9 %rev.7 = f32[128,2048]{1,0:T(8,128)} reverse(f32[128,2048]{1,0:T(8,128)} %param.17), dimensions={0} | reverse | bytes 2097152 | tf_op jit(solution)/shard_map/rev | solution.py:32
  282.3 61.5 %collective-permute-done.2 = bf16[3,256,2048]{2,1,0:T(8,128)(2,1)} collective-permute-done((bf16[3,256,2048]{2,1,0:T(8,128)(2,1)}, bf16[3,256,2048]{2,1,0:T(8,128)(2,1)}, u32[]{:S(2)}, u32[]{:S(2)}) %collective-permute-start.2) | collective-permute-done | bytes 3145760 | tf_op jit(solution)/shard_map/ppermute | solution.py:14
  343.7 4.0 constant_dynamic-update-slice_fusion.7
  347.7 4.1 constant_dynamic-update-slice_fusion.6
  351.8 2.1 constant_dynamic-update-slice_fusion.5
  353.9 1.9 constant_dynamic-update-slice_fusion.4
  355.7 3.9 constant_dynamic-update-slice_fusion.3
  359.7 3.9 constant_dynamic-update-slice_fusion.2
  363.6 2.1 constant_dynamic-update-slice_fusion.1
  365.7 1.9 constant_dynamic-update-slice_fusion
  367.6 0.7 copy-done.3
  368.3 0.4 copy-done.8
  368.7 33.7 %add_convert_fusion = bf16[3,256,2048]{2,1,0:T(8,128)(2,1)S(1)} fusion(bf16[8192,2048]{1,0:T(8,128)(2,1)} %param.15, bf16[3,256,16384]{2,1,0:T(8,128)(2,1)} %constant_dynamic-update-slice_fusion, s32[]{:T(128)S(6)} %select_n.18, bf16[1,256,2048]{2,1,0:T(8,128)(2,1)S(1)} %bitcast.32, bf16[2,256,2048]{2,1,0:T(8,128)(2,1)S(1)} %copy-done.3), kind=kOutput, calls=%fused_computation.25 | convolution fusion | flops 25776095232 | bytes 52428804 | tf_op jit(solution)/shard_map/rlk,kc->rlc/dot_general | solution.py:65
  402.4 0.1 slice_bitcast_fusion
  402.5 0.4 fusion.38
  402.9 3.5 fusion.24
  406.4 45.4 %fusion.32 = f32[2,256,2048]{2,0,1:T(2,128)S(1)} fusion(f32[2,256,2048]{2,1,0:T(8,128)S(1)} %fusion.24, f32[128,1,2048]{2,0,1:T(8,128)S(1)} %bitcast.33), kind=kOutput, calls=%fused_computation.47 | convolution fusion | flops 1211105280 | bytes 9437184 | tf_op jit(solution)/shard_map/conv_general_dilated | solution.py:33
  451.8 4.1 fusion.31
  (30 shorter events, 0.1 us)
Async XLA Ops:
  0.0 11.7 %copy-start = (bf16[2,32,2048]{2,1,0:T(8,128)(2,1)S(1)}, bf16[2,32,2048]{2,1,0:T(8,128)(2,1)}, u32[]{:S(2)}) copy-start(bf16[2,32,2048]{2,1,0:T(8,128)(2,1)} %param.10) | copy-start | bytes 786436
  0.0 11.7 %copy-start.12 = (s32[2,32]{1,0:T(2,128)S(1)}, s32[2,32]{1,0:T(2,128)}, u32[]{:S(2)}) copy-start(s32[2,32]{1,0:T(2,128)} %param.11) | copy-start | bytes 772
  1.2 11.4 %copy-start.6 = (bf16[256,2048]{1,0:T(8,128)(2,1)S(1)}, bf16[256,2048]{1,0:T(8,128)(2,1)}, u32[]{:S(2)}) copy-start(bf16[256,2048]{1,0:T(8,128)(2,1)} %param.9) | copy-start | bytes 3145732
  12.6 110.5 %copy-start.2 = (bf16[2,256,2048]{2,1,0:T(8,128)(2,1)}, bf16[2,256,2048]{2,1,0:T(8,128)(2,1)S(1)}, u32[]{:S(2)}) copy-start(bf16[2,256,2048]{2,1,0:T(8,128)(2,1)S(1)} %add_convert_fusion.1) | copy-start | bytes 6291460
  13.0 6.3 %copy-start.10 = (f32[128,2048]{1,0:T(8,128)S(1)}, f32[128,2048]{1,0:T(8,128)}, u32[]{:S(2)}) copy-start(f32[128,2048]{1,0:T(8,128)} %rev.6) | copy-start | bytes 3145732
  19.4 103.7 %copy-start.7 = (bf16[256,2048]{1,0:T(8,128)(2,1)S(1)}, bf16[256,2048]{1,0:T(8,128)(2,1)}, u32[]{:S(2)}) copy-start(bf16[256,2048]{1,0:T(8,128)(2,1)} %param.9) | copy-start | bytes 3145732
  123.1 150.2 %copy-start.13 = (s32[2,2]{1,0:T(2,128)S(1)}, s32[2,2]{1,0:T(2,128)}, u32[]{:S(2)}) copy-start(s32[2,2]{1,0:T(2,128)} %param.12) | copy-start | bytes 52
  123.1 159.1 %copy-start.11 = (f32[7,2048]{1,0:T(8,128)S(1)}, f32[7,2048]{1,0:T(8,128)}, u32[]{:S(2)}) copy-start(f32[7,2048]{1,0:T(8,128)} %param.16) | copy-start | bytes 172036
  127.2 73.2 %collective-permute-start = (bf16[3,256,2048]{2,1,0:T(8,128)(2,1)S(1)}, bf16[3,256,2048]{2,1,0:T(8,128)(2,1)S(1)}, u32[]{:S(2)}, u32[]{:S(2)}) collective-permute-start(bf16[3,256,2048]{2,1,0:T(8,128)(2,1)S(1)} %fusion.17), channel_id=1, source_target_pairs={{0,1},{1,2},{2,3},{3,0},{4,5},{5,6},{6,7},{7,4},{8,9},{9,10},{10,1... | collective-permute-start | bytes 9437192 | tf_op jit(solution)/shard_map/ppermute | solution.py:14
  200.4 1.6 copy-start.4
  202.1 71.2 %collective-permute-start.1 = (bf16[3,256,2048]{2,1,0:T(8,128)(2,1)S(1)}, bf16[3,256,2048]{2,1,0:T(8,128)(2,1)}, u32[]{:S(2)}, u32[]{:S(2)}) collective-permute-start(bf16[3,256,2048]{2,1,0:T(8,128)(2,1)S(1)} %collective-permute-done), channel_id=1, source_target_pairs={{0,1},{1,2},{2,3},{3,0},{4,5},{5,6},{6,7},{7,4},{8,9},{9,10},{10,1... | collective-permute-start | bytes 9437192 | tf_op jit(solution)/shard_map/ppermute | solution.py:14
  273.3 70.5 %collective-permute-start.2 = (bf16[3,256,2048]{2,1,0:T(8,128)(2,1)}, bf16[3,256,2048]{2,1,0:T(8,128)(2,1)}, u32[]{:S(2)}, u32[]{:S(2)}) collective-permute-start(bf16[3,256,2048]{2,1,0:T(8,128)(2,1)} %collective-permute-done.1), channel_id=1, source_target_pairs={{0,1},{1,2},{2,3},{3,0},{4,5},{5,6},{6,7},{7,4},{8,9},{9,10},{10,1... | collective-permute-start | bytes 9437192 | tf_op jit(solution)/shard_map/ppermute | solution.py:14
  347.7 4.1 copy-start.5
  365.7 2.6 copy-start.3
  365.7 3.0 copy-start.8
  402.9 3.5 copy-start.9
  406.4 49.5 %copy-start.1 = (bf16[2,32,2048]{2,1,0:T(8,128)(2,1)S(1)}, bf16[2,32,2048]{2,1,0:T(8,128)(2,1)}, u32[]{:S(2)}) copy-start(bf16[2,32,2048]{2,1,0:T(8,128)(2,1)} %param.10) | copy-start | bytes 786436
